TPU v7x, 256 devices: a whole 4x4x8 slice. The times are simulated.
256 devices in a mesh: dp: 32 (over z, x), tensor: 8 (over y, core).
Axes of the slice: x: 4, y: 4, z: 8, core: 2. Of those that a mesh axis runs over, the one named last changes fastest.
Arguments:
- activations: bfloat16 [28672, 4096], P('dp', 'tensor'), may hold values from -6 to 6
- out_grads: bfloat16 [28672, 4096], P('dp', 'tensor'), may hold values from -6 to 6
- gate_act: bfloat16 [28672, 14336], P('dp', 'tensor'), may hold values from -6 to 6
- w_down: bfloat16 [14336, 4096], P('tensor', 'dp'), may hold values from -0.09375 to 0.09375
- proj_in: bfloat16 [4096, 64], P('tensor'), may hold values from -0.09375 to 0.09375
- proj_out: bfloat16 [14336, 64], P('tensor'), may hold values from -0.046875 to 0.046875
- lengths: int32 [32, 8], P('dp'), may hold values from 1 to 448, 896 in all within a row
- assign: int32 [256], replicated, may hold values from 0 to 255, each once
Outputs:
- loggrads: float32 [256, 64, 64], P('dp', 'tensor')
Inputs may be any that keep to these rules, and one draw needn't show every extreme that they name: `lengths`: each row gives the token counts of the 8 sequences packed into one data group's 896 rows and sums to 896. `assign`: a permutation of the sequence numbers.
All inputs are finite; a program needn't handle non-finite values.
Results may differ from a plain program's by a relative error of at most 0.013.
Values may be sent and summed in bfloat16 or wider, within the bound.
No kernel may reach another device: no remote copies, remote signals or barrier semaphores. Data moves between devices by JAX's collectives and lax.ppermute only.
A program may use at most 128 MiB of HBM per device.

v0:
```python
import jax
import jax.numpy as jnp
from jax import lax
from jax.sharding import PartitionSpec as P


def member_of(seq_lengths, tok_rows):
    slots = seq_lengths.shape[0]
    before = lax.iota(jnp.int32, slots)[None, :] < lax.iota(jnp.int32, slots)[:, None]
    starts = jnp.sum(jnp.where(before, seq_lengths[None, :], 0), axis=1)
    ends = starts + seq_lengths
    positions = lax.iota(jnp.int32, tok_rows)
    inside = (positions[None, :] >= starts[:, None]) & (positions[None, :] < ends[:, None])
    return jnp.where(inside, 1.0 / seq_lengths[:, None].astype(jnp.float32), 0.0)


def place(result, assign):
    slots, values = result.shape
    groups = lax.axis_size("dp")
    mine = lax.dynamic_slice_in_dim(assign, lax.axis_index("dp") * slots, slots, 0)
    placing = (mine[None, :] == lax.iota(jnp.int32, slots * groups)[:, None]).astype(jnp.bfloat16)
    spread = jnp.dot(placing, result, preferred_element_type=jnp.float32).astype(jnp.bfloat16)
    got = lax.all_to_all(spread, "dp", split_axis=0, concat_axis=0, tiled=True)
    return jnp.sum(got.reshape(groups, slots, values).astype(jnp.float32), axis=0)


def shards(activations, out_grads, gate_act, w_down, proj_in, proj_out, lengths, assign):
    tok_rows = activations.shape[0]
    rank_all = proj_in.shape[1]
    shard_count = lax.axis_size("tensor")
    slots = lengths.shape[1]
    cols = rank_all // shard_count
    in_part = jnp.dot(activations, proj_in, preferred_element_type=jnp.float32)
    in_high = in_part.astype(jnp.bfloat16)
    in_low = (in_part - in_high.astype(jnp.float32)).astype(jnp.bfloat16)
    full_grads = lax.all_gather(out_grads, "tensor", axis=1, tiled=True)
    in_all = lax.all_gather(jnp.concatenate([in_high, in_low], axis=1), "tensor", axis=0)
    in_all = jnp.sum(in_all.astype(jnp.float32), axis=0)
    in_sum = in_all[:, :rank_all] + in_all[:, rank_all:]
    weighted = member_of(lengths[0], tok_rows)[:, :, None] * in_sum[None, :, :]
    hidden_grad = lax.dot_general(
        full_grads,
        lax.all_gather(w_down, "dp", axis=1, tiled=True),
        (((1,), (1,)), ((), ())),
        preferred_element_type=jnp.float32,
    )
    up_grad = (hidden_grad * gate_act.astype(jnp.float32)).astype(jnp.bfloat16)
    out_part = jnp.dot(up_grad, proj_out, preferred_element_type=jnp.float32)
    part = jnp.einsum("ctp,tq->cpq", weighted, out_part, precision=lax.Precision.HIGHEST)
    part = part.reshape(slots, shard_count, cols * rank_all).transpose(1, 0, 2)
    result = jnp.sum(
        lax.all_to_all(part, "tensor", split_axis=0, concat_axis=0, tiled=True), axis=0
    )
    return place(result.astype(jnp.bfloat16), assign).reshape(slots, cols, rank_all)


def solution(mesh):
    in_specs = (
        P("dp", "tensor"),
        P("dp", "tensor"),
        P("dp", "tensor"),
        P("tensor", "dp"),
        P("tensor", None),
        P("tensor", None),
        P("dp", None),
        P(),
    )
    out_specs = P("dp", "tensor", None)
    return jax.shard_map(shards, mesh=mesh, in_specs=in_specs, out_specs=out_specs, check_vma=False)
```

profile of v0, /device:TPU:32, one launch (start us, length us, event | category | flops | bytes accessed | tf_op | source)
XLA Modules:
  0.0 291.1 jit_solution(1241002359419916471)
XLA Ops:
  6.5 0.0 copy-start
  6.5 0.0 all-gather.9.cloned.1.call-start
  6.5 1.2 copy-done
  7.7 1.3 subtract_convert_fusion
  9.0 0.7 pad_maximum_fusion
  9.7 0.0 all-gather.9.cloned.1.call-update
  9.7 0.0 all-gather.5.cloned.1.call-start
  9.8 0.7 all-gather.5.cloned.1.call-update
  10.5 0.0 all-gather.7.cloned.1.call-start
  10.5 0.7 all-gather.7.cloned.1.call-update
  11.2 0.8 select_reduce_fusion
  12.0 0.7 convert_divide_fusion
  12.7 0.7 bitcast_add_fusion
  13.3 0.1 fusion.9
  13.4 26.7 %all-gather.9.cloned.1.call-done = bf16[7168,128]{0,1:T(8,128)(2,1)} async-done(((bf16[896,128]{0,1:T(8,128)(2,1)}), bf16[7168,128]{0,1:T(8,128)(2,1)}) %all-gather.9.cloned.1.call-update) | async-done | bytes 1835024 | tf_op jit(solution)/shard_map/all_gather | solution.py:37
  40.1 1.9 convert_element_type.46
  42.0 0.0 copy-start.1
  42.0 0.6 copy.11
  42.7 0.9 bitcast_reduce_fusion
  43.6 0.0 copy-start.2
  43.6 46.3 %all-gather.5.cloned.1.call-done = bf16[896,4096]{1,0:T(8,128)(2,1)} async-done(((bf16[896,512]{1,0:T(8,128)(2,1)}), bf16[896,4096]{1,0:T(8,128)(2,1)}) %all-gather.5.cloned.1.call-update) | async-done | bytes 7340048 | tf_op jit(solution)/shard_map/all_gather | solution.py:36
  89.8 141.1 %all-gather.7.cloned.1.call-done = bf16[1792,4096]{1,0:T(8,128)(2,1)} async-done(((bf16[1792,128]{1,0:T(8,128)(2,1)}), bf16[1792,4096]{1,0:T(8,128)(2,1)}) %all-gather.7.cloned.1.call-update) | async-done | bytes 14680080 | tf_op jit(solution)/shard_map/all_gather | solution.py:43
  230.9 0.0 copy-done.1
  230.9 22.0 %fusion.4 = f32[896,64,1]{0,1,2:T(8,128)S(1)} fusion(bf16[1792,64]{0,1:T(8,128)(2,1)S(1)} %copy-done.1, bf16[896,1792]{1,0:T(8,128)(2,1)} %param.10, bf16[896,4096]{1,0:T(8,128)(2,1)} %all-gather.5.cloned.1.call-done, bf16[1792,4096]{1,0:T(8,128)(2,1)} %all-gather.7.cloned.1.call-done), kind=kOutput, calls=%fused_computation.7 | convolution fusion | flops 13363675136 | bytes 25690112 | tf_op jit(solution)/shard_map/dot_general | solution.py:48
  253.0 1.7 fusion.1
  254.6 0.1 reshape.85
  254.8 0.7 copy.13
  255.5 4.3 %all-to-all-start = ((f32[8,8,512]{2,1,0:T(8,128)}), f32[8,8,512]{2,1,0:T(8,128)S(1)}, u32[]{:S(2)}, u32[]{:S(2)}) async-start(f32[8,8,512]{2,1,0:T(8,128)} %bitcast.21), calls=%async_computation | async-start | bytes 262144 | tf_op jit(solution)/shard_map/all_to_all | solution.py:52
  259.8 0.0 copy-done.2
  259.8 0.1 dynamic_slice.3
  259.8 6.1 %all-to-all-done = f32[8,8,512]{2,1,0:T(8,128)S(1)} async-done(((f32[8,8,512]{2,1,0:T(8,128)}), f32[8,8,512]{2,1,0:T(8,128)S(1)}, u32[]{:S(2)}, u32[]{:S(2)}) %all-to-all-start) | async-done | bytes 131104 | tf_op jit(solution)/shard_map/all_to_all | solution.py:52
  265.9 0.2 fusion.3
  266.1 17.7 %all_to_all.14 = bf16[32,8,512]{2,1,0:T(8,128)(2,1)S(1)} all-to-all(bf16[32,8,512]{2,1,0:T(8,128)(2,1)S(1)} %fusion.3), channel_id=1, replica_groups=mesh['dp'=32,'tensor'=8] {'dp'}, dimensions={0} | all-to-all | bytes 524288 | tf_op jit(solution)/shard_map/all_to_all | solution.py:23
  283.9 0.7 reshape.86
  (3 shorter events, 0.1 us)
Async XLA Ops:
  6.5 1.2 copy-start
  6.5 33.6 %all-gather.9.cloned.1.call-start = ((), (), s32[]{:S(2)}) async-start(), calls=%async_computation.4 | async-start | bytes 2064384 | tf_op jit(solution)/shard_map/all_gather | solution.py:37
  9.7 80.1 %all-gather.5.cloned.1.call-start = ((), (), s32[]{:S(2)}) async-start(), calls=%async_computation.2 | async-start | bytes 8257536 | tf_op jit(solution)/shard_map/all_gather | solution.py:36
  10.5 220.4 %all-gather.7.cloned.1.call-start = ((), (), s32[]{:S(2)}) async-start(), calls=%async_computation.3 | async-start | bytes 15138816 | tf_op jit(solution)/shard_map/all_gather | solution.py:43
  42.0 188.9 %copy-start.1 = (bf16[1792,64]{0,1:T(8,128)(2,1)S(1)}, bf16[1792,64]{0,1:T(8,128)(2,1)}, u32[]{:S(2)}) copy-start(bf16[1792,64]{0,1:T(8,128)(2,1)} %param.13) | copy-start | bytes 688132
  43.6 216.2 %copy-start.2 = (s32[256]{0:T(256)S(1)}, s32[256]{0:T(256)}, u32[]{:S(2)}) copy-start(s32[256]{0:T(256)} %param.15) | copy-start | bytes 3076
  255.5 10.4 %all-to-all-start = ((f32[8,8,512]{2,1,0:T(8,128)}), f32[8,8,512]{2,1,0:T(8,128)S(1)}, u32[]{:S(2)}, u32[]{:S(2)}) async-start(f32[8,8,512]{2,1,0:T(8,128)} %bitcast.21), calls=%async_computation | async-start | bytes 262144 | tf_op jit(solution)/shard_map/all_to_all | solution.py:52
Sparse Core Ops, SparseCore 0:
  9.9 30.2 all-gather.8
  42.0 47.8 all-gather.4
  92.3 138.5 all-gather.6
where the time goes:
time: 291 us
  waiting for transfers between devices  222 us (76%)
  matrix products  25.2 us (9%)
  blocking collectives  17.7 us (6%)
  between operations  13.2 us (5%)
  other arithmetic  5.72 us (2%)
  starting transfers between devices  4.37 us (2%)
  local copies, waits for them, and re-layouts  3.43 us (1%)
    all_gather x1, waiting for transfers between devices, shards(): lax.all_gather(w_down, 'dp', axis=1, tiled=True)  141 us
    all_gather x1, waiting for transfers between devices, shards(): full_grads = lax.all_gather(out_grads, 'tensor', axis=1, tiled=True)  46.3 us
    all_gather x1, waiting for transfers between devices, shards(): lax.all_gather(jnp.concatenate([in_high, in_low], axis=1), 'tensor', axis=0)  26.7 us
    dot_general x1, matrix products, shards(): out_part = jnp.dot(up_grad, proj_out, preferred_element_type=jnp.float32)  22 us
    all_to_all x1, blocking collectives, place(): got = lax.all_to_all(spread, 'dp', split_axis=0, concat_axis=0, tiled=True)  17.7 us
    all_to_all x1, waiting for transfers between devices, shards(): lax.all_to_all(part, 'tensor', split_axis=0, concat_axis=0, tiled=True)  6.05 us
  transfers between devices with their start and end apart: 4, of which 4 were waited for; matrix products, arithmetic and copies ran while one was open for 2% of the time, Pallas kernels for 0%

commit v1 on v0

--- a/solution.py
+++ b/solution.py
@@ -2,6 +2,17 @@
 import jax.numpy as jnp
 from jax import lax
 from jax.sharding import PartitionSpec as P
+
+
+def around_the_ring(block, name, along):
+    count = lax.axis_size(name)
+    forward = [(i, (i + 1) % count) for i in range(count)]
+    parts = [block]
+    for hop in range(1, count):
+        parts = [lax.ppermute(parts[0], name, forward), *parts]
+    full = jnp.concatenate(parts, axis=along)
+    shift = (lax.axis_index(name) + 1) * parts[-1].shape[along]
+    return jnp.roll(full, shift, axis=along)
 
 
 def member_of(seq_lengths, tok_rows):
@@ -33,7 +44,7 @@
     in_part = jnp.dot(activations, proj_in, preferred_element_type=jnp.float32)
     in_high = in_part.astype(jnp.bfloat16)
     in_low = (in_part - in_high.astype(jnp.float32)).astype(jnp.bfloat16)
-    full_grads = lax.all_gather(out_grads, "tensor", axis=1, tiled=True)
+    full_grads = around_the_ring(out_grads, "tensor", 1)
     in_all = lax.all_gather(jnp.concatenate([in_high, in_low], axis=1), "tensor", axis=0)
     in_all = jnp.sum(in_all.astype(jnp.float32), axis=0)
     in_sum = in_all[:, :rank_all] + in_all[:, rank_all:]

time: 291 us -> 243 us (0.84)
  waiting for transfers between devices: 222 us -> 147 us
  local copies, waits for them, and re-layouts: 3.43 us -> 29.2 us
    all_gather x1, waiting for transfers between devices: 141 us -> 39.6 us  [shards(): lax.all_gather(w_down, 'dp', axis=1, tiled=True)]
    ppermute x0 -> x7, waiting for transfers between devices: none -> 100 us  [around_the_ring(): parts = [lax.ppermute(parts[0], name, forward), *parts]]
    all_gather x1 -> x0, waiting for transfers between devices: 46.3 us -> none  [shards(): full_grads = lax.all_gather(out_grads, 'tensor', axis=1, tiled=True)]
    all_gather x1, waiting for transfers between devices: 26.7 us -> 0.01 us  [shards(): lax.all_gather(jnp.concatenate([in_high, in_low], axis=1), 'tensor', axis=0)]
    unnamed x7 -> x36, local copies, waits for them, and re-layouts: 1.83 us -> 26.6 us
  transfers between devices with their start and end apart: 4 -> 10, of which waited for: 4 -> 9; matrix products, arithmetic and copies ran while one was open for 2% -> 12% of each run, Pallas kernels for 0% -> 0%
where the time goes in v1:
time: 243 us; the launch traced here: 242 us
  waiting for transfers between devices  147 us (60%)
  local copies, waits for them, and re-layouts  29.2 us (12%)
  matrix products  25.1 us (10%)
  blocking collectives  17.7 us (7%)
  between operations  13.5 us (6%)
  other arithmetic  5.88 us (2%)
  starting transfers between devices  4.37 us (2%)
    ppermute x7, waiting for transfers between devices, around_the_ring(): parts = [lax.ppermute(parts[0], name, forward), *parts]  100 us
    all_gather x1, waiting for transfers between devices, shards(): lax.all_gather(w_down, 'dp', axis=1, tiled=True)  39.6 us
    unnamed x36, local copies, waits for them, and re-layouts  26.6 us
    dot_general x1, matrix products, shards(): out_part = jnp.dot(up_grad, proj_out, preferred_element_type=jnp.float32)  22 us
    all_to_all x1, blocking collectives, place(): got = lax.all_to_all(spread, 'dp', split_axis=0, concat_axis=0, tiled=True)  17.7 us
    all_to_all x1, waiting for transfers between devices, shards(): lax.all_to_all(part, 'tensor', split_axis=0, concat_axis=0, tiled=True)  6.05 us
  transfers between devices with their start and end apart: 10, of which 9 were waited for; matrix products, arithmetic and copies ran while one was open for 12% of the time, Pallas kernels for 0%

profile of v1, /device:TPU:32, one launch (start us, length us, event | category | flops | bytes accessed | tf_op | source)
XLA Modules:
  0.0 242.3 jit_solution(3343884244185471683)
XLA Ops:
  6.5 1.2 copy-done
  7.7 1.3 subtract_convert_fusion
  9.0 0.7 pad_maximum_fusion
  9.7 0.0 all-gather.4.cloned.1.call-start
  9.8 0.7 all-gather.4.cloned.1.call-update
  10.5 14.2 %collective-permute-done = bf16[896,512]{1,0:T(8,128)(2,1)S(1)} collective-permute-done((bf16[896,512]{1,0:T(8,128)(2,1)}, bf16[896,512]{1,0:T(8,128)(2,1)S(1)}, u32[]{:S(2)}, u32[]{:S(2)}) %collective-permute-start) | collective-permute-done | bytes 917536 | tf_op jit(solution)/shard_map/ppermute | solution.py:12
  24.7 20.9 %collective-permute-done.1 = bf16[896,512]{1,0:T(8,128)(2,1)S(1)} collective-permute-done((bf16[896,512]{1,0:T(8,128)(2,1)S(1)}, bf16[896,512]{1,0:T(8,128)(2,1)S(1)}, u32[]{:S(2)}, u32[]{:S(2)}) %collective-permute-start.1) | collective-permute-done | bytes 917536 | tf_op jit(solution)/shard_map/ppermute | solution.py:12
  45.6 14.0 %collective-permute-done.2 = bf16[896,512]{1,0:T(8,128)(2,1)S(1)} collective-permute-done((bf16[896,512]{1,0:T(8,128)(2,1)S(1)}, bf16[896,512]{1,0:T(8,128)(2,1)S(1)}, u32[]{:S(2)}, u32[]{:S(2)}) %collective-permute-start.2) | collective-permute-done | bytes 917536 | tf_op jit(solution)/shard_map/ppermute | solution.py:12
  59.7 1.0 copy-done.4
  60.6 14.0 %collective-permute-done.3 = bf16[896,512]{1,0:T(8,128)(2,1)S(1)} collective-permute-done((bf16[896,512]{1,0:T(8,128)(2,1)S(1)}, bf16[896,512]{1,0:T(8,128)(2,1)S(1)}, u32[]{:S(2)}, u32[]{:S(2)}) %collective-permute-start.3) | collective-permute-done | bytes 917536 | tf_op jit(solution)/shard_map/ppermute | solution.py:12
  74.7 0.9 copy-done.6
  75.6 14.1 %collective-permute-done.4 = bf16[896,512]{1,0:T(8,128)(2,1)} collective-permute-done((bf16[896,512]{1,0:T(8,128)(2,1)S(1)}, bf16[896,512]{1,0:T(8,128)(2,1)}, u32[]{:S(2)}, u32[]{:S(2)}) %collective-permute-start.4) | collective-permute-done | bytes 917536 | tf_op jit(solution)/shard_map/ppermute | solution.py:12
  89.7 0.8 select_reduce_fusion
  90.5 0.7 bitcast_add_fusion
  91.2 12.9 %collective-permute-done.5 = bf16[896,512]{1,0:T(8,128)(2,1)} collective-permute-done((bf16[896,512]{1,0:T(8,128)(2,1)}, bf16[896,512]{1,0:T(8,128)(2,1)}, u32[]{:S(2)}, u32[]{:S(2)}) %collective-permute-start.5) | collective-permute-done | bytes 917536 | tf_op jit(solution)/shard_map/ppermute | solution.py:12
  104.1 0.7 convert_divide_fusion
  104.7 0.1 fusion.17
  104.9 2.0 convert_element_type.46
  106.9 0.6 copy.11
  107.6 0.9 bitcast_reduce_fusion
  108.5 9.9 %collective-permute-done.6 = bf16[896,512]{1,0:T(8,128)(2,1)} collective-permute-done((bf16[896,512]{1,0:T(8,128)(2,1)}, bf16[896,512]{1,0:T(8,128)(2,1)}, u32[]{:S(2)}, u32[]{:S(2)}) %collective-permute-start.6) | collective-permute-done | bytes 917536 | tf_op jit(solution)/shard_map/ppermute | solution.py:12
  118.4 2.3 constant_dynamic-update-slice_fusion.15
  120.7 2.2 constant_dynamic-update-slice_fusion.14
  122.9 2.2 constant_dynamic-update-slice_fusion.13
  125.1 1.1 constant_dynamic-update-slice_fusion.12
  126.2 1.0 constant_dynamic-update-slice_fusion.11
  127.2 1.1 constant_dynamic-update-slice_fusion.10
  128.3 1.1 constant_dynamic-update-slice_fusion.9
  129.3 1.1 constant_dynamic-update-slice_fusion.8
  130.4 2.3 constant_dynamic-update-slice_fusion.7
  132.7 2.3 constant_dynamic-update-slice_fusion.6
  135.0 2.2 constant_dynamic-update-slice_fusion.5
  137.2 1.0 constant_dynamic-update-slice_fusion.4
  138.2 1.0 constant_dynamic-update-slice_fusion.3
  139.2 1.0 constant_dynamic-update-slice_fusion.2
  140.2 1.0 constant_dynamic-update-slice_fusion.1
  141.2 1.0 constant_dynamic-update-slice_fusion
  142.3 39.6 %all-gather.4.cloned.1.call-done = bf16[1792,4096]{1,0:T(8,128)(2,1)} async-done(((bf16[1792,128]{1,0:T(8,128)(2,1)}), bf16[1792,4096]{1,0:T(8,128)(2,1)}) %all-gather.4.cloned.1.call-update) | async-done | bytes 14680080 | tf_op jit(solution)/shard_map/all_gather | solution.py:54
  181.9 22.0 %fusion.10 = f32[896,64,1]{0,1,2:T(8,128)S(1)} fusion(bf16[1792,64]{0,1:T(8,128)(2,1)S(1)} %copy-done.8, bf16[896,1792]{1,0:T(8,128)(2,1)} %param.10, bf16[1792,4096]{1,0:T(8,128)(2,1)} %all-gather.4.cloned.1.call-done, bf16[896,8192]{1,0:T(8,128)(2,1)} %constant_dynamic-update-slice_fusion, s32[]{:T(128)S(6)} %select_n.32), kind=kOutput, calls=%fused_computation.9 | convolution fusion | flops 13363675136 | bytes 25690116 | tf_op jit(solution)/shard_map/dot_general | solution.py:59
  203.9 1.6 fusion.7
  205.6 0.1 reshape.85
  205.7 0.7 copy.13
  206.4 4.3 %all-to-all-start = ((f32[8,8,512]{2,1,0:T(8,128)}), f32[8,8,512]{2,1,0:T(8,128)S(1)}, u32[]{:S(2)}, u32[]{:S(2)}) async-start(f32[8,8,512]{2,1,0:T(8,128)} %bitcast.20), calls=%async_computation | async-start | bytes 262144 | tf_op jit(solution)/shard_map/all_to_all | solution.py:63
  210.7 0.1 dynamic_slice.7
  210.8 6.1 %all-to-all-done = f32[8,8,512]{2,1,0:T(8,128)S(1)} async-done(((f32[8,8,512]{2,1,0:T(8,128)}), f32[8,8,512]{2,1,0:T(8,128)S(1)}, u32[]{:S(2)}, u32[]{:S(2)}) %all-to-all-start) | async-done | bytes 131104 | tf_op jit(solution)/shard_map/all_to_all | solution.py:63
  216.8 0.2 fusion.9
  217.1 17.7 %all_to_all.14 = bf16[32,8,512]{2,1,0:T(8,128)(2,1)S(1)} all-to-all(bf16[32,8,512]{2,1,0:T(8,128)(2,1)S(1)} %fusion.9), channel_id=1, replica_groups=mesh['dp'=32,'tensor'=8] {'dp'}, dimensions={0} | all-to-all | bytes 524288 | tf_op jit(solution)/shard_map/all_to_all | solution.py:34
  234.8 0.7 reshape.86
  (30 shorter events, 0.2 us)
Async XLA Ops:
  6.5 1.2 copy-start
  6.5 98.3 %all-gather.6.cloned.1.call-start = ((), (), s32[]{:S(2)}) async-start(), calls=%async_computation.3 | async-start | bytes 2064384 | tf_op jit(solution)/shard_map/all_gather | solution.py:48
  9.7 172.2 %all-gather.4.cloned.1.call-start = ((), (), s32[]{:S(2)}) async-start(), calls=%async_computation.2 | async-start | bytes 15138816 | tf_op jit(solution)/shard_map/all_gather | solution.py:54
  10.5 14.3 %collective-permute-start = (bf16[896,512]{1,0:T(8,128)(2,1)}, bf16[896,512]{1,0:T(8,128)(2,1)S(1)}, u32[]{:S(2)}, u32[]{:S(2)}) collective-permute-start(bf16[896,512]{1,0:T(8,128)(2,1)} %param.9), channel_id=1, source_target_pairs={{0,1},{1,2},{2,3},{3,4},{4,5},{5,6},{6,7},{7,0},{8,9},{9,10},{10,1... | collective-permute-start | bytes 2752520 | tf_op jit(solution)/shard_map/ppermute | solution.py:12
  24.7 20.9 %collective-permute-start.1 = (bf16[896,512]{1,0:T(8,128)(2,1)S(1)}, bf16[896,512]{1,0:T(8,128)(2,1)S(1)}, u32[]{:S(2)}, u32[]{:S(2)}) collective-permute-start(bf16[896,512]{1,0:T(8,128)(2,1)S(1)} %collective-permute-done), channel_id=1, source_target_pairs={{0,1},{1,2},{2,3},{3,4},{4,5},{5,6},{6,7},{7,0},{8,9},{9,10},{10,1... | collective-permute-start | bytes 2752520 | tf_op jit(solution)/shard_map/ppermute | solution.py:12
  45.6 59.1 %copy-start.2 = (bf16[896,512]{1,0:T(8,128)(2,1)}, bf16[896,512]{1,0:T(8,128)(2,1)S(1)}, u32[]{:S(2)}) copy-start(bf16[896,512]{1,0:T(8,128)(2,1)S(1)} %collective-permute-done.1) | copy-start | bytes 2752516
  45.6 14.0 %collective-permute-start.2 = (bf16[896,512]{1,0:T(8,128)(2,1)S(1)}, bf16[896,512]{1,0:T(8,128)(2,1)S(1)}, u32[]{:S(2)}, u32[]{:S(2)}) collective-permute-start(bf16[896,512]{1,0:T(8,128)(2,1)S(1)} %collective-permute-done.1), channel_id=1, source_target_pairs={{0,1},{1,2},{2,3},{3,4},{4,5},{5,6},{6,7},{7,0},{8,9},{9,10},{10,1... | collective-permute-start | bytes 2752520 | tf_op jit(solution)/shard_map/ppermute | solution.py:12
  59.7 1.0 copy-start.4
  60.6 14.0 %collective-permute-start.3 = (bf16[896,512]{1,0:T(8,128)(2,1)S(1)}, bf16[896,512]{1,0:T(8,128)(2,1)S(1)}, u32[]{:S(2)}, u32[]{:S(2)}) collective-permute-start(bf16[896,512]{1,0:T(8,128)(2,1)S(1)} %collective-permute-done.2), channel_id=1, source_target_pairs={{0,1},{1,2},{2,3},{3,4},{4,5},{5,6},{6,7},{7,0},{8,9},{9,10},{10,1... | collective-permute-start | bytes 2752520 | tf_op jit(solution)/shard_map/ppermute | solution.py:12
  74.6 0.9 copy-start.6
  75.6 14.1 %collective-permute-start.4 = (bf16[896,512]{1,0:T(8,128)(2,1)S(1)}, bf16[896,512]{1,0:T(8,128)(2,1)}, u32[]{:S(2)}, u32[]{:S(2)}) collective-permute-start(bf16[896,512]{1,0:T(8,128)(2,1)S(1)} %collective-permute-done.3), channel_id=1, source_target_pairs={{0,1},{1,2},{2,3},{3,4},{4,5},{5,6},{6,7},{7,0},{8,9},{9,10},{10,1... | collective-permute-start | bytes 2752520 | tf_op jit(solution)/shard_map/ppermute | solution.py:12
  89.7 14.3 %collective-permute-start.5 = (bf16[896,512]{1,0:T(8,128)(2,1)}, bf16[896,512]{1,0:T(8,128)(2,1)}, u32[]{:S(2)}, u32[]{:S(2)}) collective-permute-start(bf16[896,512]{1,0:T(8,128)(2,1)} %collective-permute-done.4), channel_id=1, source_target_pairs={{0,1},{1,2},{2,3},{3,4},{4,5},{5,6},{6,7},{7,0},{8,9},{9,10},{10,1... | collective-permute-start | bytes 2752520 | tf_op jit(solution)/shard_map/ppermute | solution.py:12
  104.1 14.3 %collective-permute-start.6 = (bf16[896,512]{1,0:T(8,128)(2,1)}, bf16[896,512]{1,0:T(8,128)(2,1)}, u32[]{:S(2)}, u32[]{:S(2)}) collective-permute-start(bf16[896,512]{1,0:T(8,128)(2,1)} %collective-permute-done.5), channel_id=1, source_target_pairs={{0,1},{1,2},{2,3},{3,4},{4,5},{5,6},{6,7},{7,0},{8,9},{9,10},{10,1... | collective-permute-start | bytes 2752520 | tf_op jit(solution)/shard_map/ppermute | solution.py:12
  104.8 24.5 %copy-start.1 = (bf16[896,512]{1,0:T(8,128)(2,1)S(1)}, bf16[896,512]{1,0:T(8,128)(2,1)}, u32[]{:S(2)}) copy-start(bf16[896,512]{1,0:T(8,128)(2,1)} %param.9) | copy-start | bytes 2752516
  104.8 20.3 %copy-start.7 = (bf16[896,512]{1,0:T(8,128)(2,1)S(1)}, bf16[896,512]{1,0:T(8,128)(2,1)}, u32[]{:S(2)}) copy-start(bf16[896,512]{1,0:T(8,128)(2,1)} %copy-done.6) | copy-start | bytes 2752516
  104.8 21.4 %copy-start.5 = (bf16[896,512]{1,0:T(8,128)(2,1)S(1)}, bf16[896,512]{1,0:T(8,128)(2,1)}, u32[]{:S(2)}) copy-start(bf16[896,512]{1,0:T(8,128)(2,1)} %copy-done.4) | copy-start | bytes 2752516
  104.8 22.4 %copy-start.3 = (bf16[896,512]{1,0:T(8,128)(2,1)S(1)}, bf16[896,512]{1,0:T(8,128)(2,1)}, u32[]{:S(2)}) copy-start(bf16[896,512]{1,0:T(8,128)(2,1)} %copy-done.2) | copy-start | bytes 2752516
  108.5 73.4 %copy-start.8 = (bf16[1792,64]{0,1:T(8,128)(2,1)S(1)}, bf16[1792,64]{0,1:T(8,128)(2,1)}, u32[]{:S(2)}) copy-start(bf16[1792,64]{0,1:T(8,128)(2,1)} %param.13) | copy-start | bytes 688132
  142.3 68.4 %copy-start.9 = (s32[256]{0:T(256)S(1)}, s32[256]{0:T(256)}, u32[]{:S(2)}) copy-start(s32[256]{0:T(256)} %param.15) | copy-start | bytes 3076
  206.4 10.4 %all-to-all-start = ((f32[8,8,512]{2,1,0:T(8,128)}), f32[8,8,512]{2,1,0:T(8,128)S(1)}, u32[]{:S(2)}, u32[]{:S(2)}) async-start(f32[8,8,512]{2,1,0:T(8,128)} %bitcast.20), calls=%async_computation | async-start | bytes 262144 | tf_op jit(solution)/shard_map/all_to_all | solution.py:63
Sparse Core Ops, SparseCore 0:
  9.8 31.2 all-gather.5
  43.6 138.2 all-gather.3
